TPU v7x, 32 devices: a whole 2x2x4 slice. The times are simulated.
32 devices in a mesh: snap: 8 (over z, x), vert: 4 (over y, core).
Axes of the slice: x: 2, y: 2, z: 4, core: 2. Of those that a mesh axis runs over, the one named last changes fastest.
Arguments:
- features: bfloat16 [8, 1024, 512], P('snap', 'vert'), may hold values from -6 to 6
- tile_values: bfloat16 [8, 8, 12, 128, 128], P('snap', 'vert'), may hold values from -0.21875 to 0.21875
- tile_column: int32 [8, 8, 12], P('snap', 'vert'), may hold values from 0 to 7
- tile_count: int32 [8, 8], P('snap', 'vert'), may hold values from 1 to 12, 48 in all within a row
- message_one: bfloat16 [512, 512], replicated, may hold values from -0.25 to 0.25
- root_one: bfloat16 [512, 512], replicated, may hold values from -0.25 to 0.25
- time_taps: float32 [16, 512], replicated, may hold values from -1.5 to 1.5
- message_two: bfloat16 [512, 512], replicated, may hold values from -0.25 to 0.25
- root_two: bfloat16 [512, 512], replicated, may hold values from -0.25 to 0.25
Outputs:
- embedding: bfloat16 [8, 1024, 512], P('snap', 'vert')
Inputs may be any that keep to these rules, and one draw needn't show every extreme that they name: `tile_count`: over one snapshot the counts sum to 48, and some row block has 12 live slots; slots at or past the count are ignored. `tile_column`: blocks may repeat within a row block's list.
All inputs are finite; a program needn't handle non-finite values.
Results may differ from a plain program's by a relative error of at most 0.0064.
Values may be sent and summed in bfloat16 or wider, within the bound.
A program may use at most 64 MiB of HBM per device.

v0:
```python
import jax
import jax.numpy as jnp
from jax import lax
from jax.sharding import PartitionSpec as P

TILE = 128
TAPS = 16


def block_table(columns, counts, total_blocks):
    live = lax.broadcasted_iota(jnp.int32, columns.shape, 2) < counts[:, :, None]
    target = lax.broadcasted_iota(jnp.int32, columns.shape + (total_blocks,), 3)
    hits = (columns[:, :, :, None] == target) & live[:, :, :, None]
    return jnp.where(hits, 1.0, 0.0).astype(jnp.bfloat16)


def aggregate(messages, table, tile_values):
    snaps, rows, width = messages.shape
    piece = lax.all_gather(messages, "vert", axis=1, tiled=True)
    count = piece.shape[1] // TILE
    blocks = piece.reshape(snaps, count, TILE, width)
    chosen = jnp.einsum(
        "srkp,sptf->srktf", table, blocks, preferred_element_type=jnp.float32
    ).astype(jnp.bfloat16)
    summed = jnp.einsum(
        "srkij,srkjf->srif", tile_values, chosen, preferred_element_type=jnp.float32
    )
    return summed.reshape(snaps, rows, width)


def graph_layer(inputs, w_message, w_root, table, tile_values):
    messages = jnp.einsum(
        "svf,fg->svg", inputs, w_message, preferred_element_type=jnp.float32
    ).astype(jnp.bfloat16)
    summed = aggregate(messages, table, tile_values)
    total = summed + jnp.einsum("svf,fg->svg", inputs, w_root, preferred_element_type=jnp.float32)
    return jnp.maximum(total, 0.0).astype(jnp.bfloat16)


def shards(
    features,
    tile_values,
    tile_column,
    tile_count,
    message_one,
    root_one,
    time_taps,
    message_two,
    root_two,
):
    table = block_table(tile_column, tile_count, tile_column.shape[1] * lax.axis_size("vert"))
    hidden = graph_layer(features, message_one, root_one, table, tile_values)
    by_vertex = lax.all_to_all(hidden, "snap", split_axis=1, concat_axis=0, tiled=True)
    steps_all, vrows, width = by_vertex.shape
    wide = by_vertex.astype(jnp.float32)
    padded = jnp.concatenate([jnp.zeros((TAPS - 1, vrows, width), jnp.float32), wide], 0)
    mixed = jnp.zeros((steps_all, vrows, width), jnp.float32)
    for offset in range(TAPS):
        mixed = (
            mixed
            + time_taps[offset][None, None, :]
            * padded[TAPS - 1 - offset : TAPS - 1 - offset + steps_all]
        )
    mixed = mixed.astype(jnp.bfloat16)
    returned = lax.all_to_all(mixed, "snap", split_axis=0, concat_axis=1, tiled=True)
    return graph_layer(returned, message_two, root_two, table, tile_values)


def solution(mesh):
    return jax.shard_map(
        shards,
        mesh=mesh,
        in_specs=(
            P("snap", "vert", None),
            P("snap", "vert", None, None, None),
            P("snap", "vert", None),
            P("snap", "vert"),
            P(),
            P(),
            P(),
            P(),
            P(),
        ),
        out_specs=P("snap", "vert", None),
        check_vma=False,
    )
```

profile of v0, /device:TPU:1, one launch (start us, length us, event | category | flops | bytes accessed | tf_op | source)
XLA Modules:
  0.0 96.4 jit_solution(11090776534484677294)
XLA Ops:
  6.5 0.0 copy-start
  6.5 0.0 all-gather.5.cloned.1.call-start
  6.5 2.2 %convolution_convert_fusion.1 = bf16[256,512]{1,0:T(8,128)(2,1)} fusion(bf16[512,512]{1,0:T(8,128)(2,1)} %param.13, bf16[1,256,512]{2,1,0:T(8,128)(2,1)} %param.9), kind=kOutput, calls=%fused_computation.18 | convolution fusion | flops 134348800 | bytes 1048576 | tf_op jit(solution)/shard_map/svf,fg->svg/dot_general | solution.py:32
  8.7 0.0 all-gather.5.cloned.1.call-update
  8.8 0.7 iota_compare_fusion.1
  9.5 18.7 %all-gather.5.cloned.1.call-done = bf16[1024,512]{1,0:T(8,128)(2,1)} async-done(((bf16[256,512]{1,0:T(8,128)(2,1)}), bf16[1024,512]{1,0:T(8,128)(2,1)}) %all-gather.5.cloned.1.call-update) | async-done | bytes 1048592 | tf_op jit(solution)/shard_map/all_gather | solution.py:19
  28.2 0.0 copy-start.1
  28.2 0.0 copy-start.2
  28.2 2.6 %fusion.10 = bf16[2,12,128,512]{3,1,2,0:T(8,128)(2,1)S(1)} fusion(bf16[8,128,512,1]{2,1,0,3:T(8,128)(2,1)} %bitcast.74, s32[2,12]{1,0:T(2,128)} %bitcast.94, pred[2,12]{1,0:T(4,128)(4,1)S(1)} %iota_compare_fusion.1), kind=kOutput, calls=%fused_computation.23 | convolution fusion | flops 25166592 | bytes 4194424 | tf_op jit(solution)/shard_map/srkp,sptf->srktf/dot_general | solution.py:22
  30.8 0.0 copy-done
  30.8 0.0 copy-start.5
  30.8 3.5 %fusion = f32[2,512,128,1]{1,2,3,0:T(8,128)S(1)} fusion(bf16[2,12,128,512]{3,1,2,0:T(8,128)(2,1)S(1)} %fusion.10, bf16[1,2,12,128,128]{4,3,2,1,0:T(8,128)(2,1)S(1)} %copy-done), kind=kOutput, calls=%fused_computation.9 | convolution fusion | flops 402653184 | bytes 4456448 | tf_op jit(solution)/shard_map/srkij,srkjf->srif/dot_general | solution.py:25
  34.3 0.0 copy-start.4
  34.3 0.0 copy-done.1
  34.3 0.0 copy-done.2
  34.3 0.0 copy-start.6
  34.3 0.3 fusion.7
  34.6 0.4 copy.28
  35.1 0.5 broadcast.144
  35.6 2.2 %reduce = bf16[256,512]{1,0:T(8,128)(2,1)S(1)} reduce(bf16[256,1,512]{2,1,0:T(2,128)(2,1)S(1)} %bitcast.72, bf16[]{:T(256)} %broadcast.144), dimensions={1}, to_apply=%bitcast.68.reduce_sub_computation | reduce | bytes 524290
  37.8 0.9 reshape.177
  38.7 5.2 %all-to-all-start = ((bf16[8,2,8192]{2,1,0:T(2,128)(2,1)}), bf16[8,2,8192]{2,1,0:T(2,128)(2,1)S(1)}, u32[]{:S(2)}, u32[]{:S(2)}) async-start(bf16[8,2,8192]{2,1,0:T(2,128)(2,1)} %reshape.177), calls=%async_computation | async-start | bytes 524288 | tf_op jit(solution)/shard_map/all_to_all | solution.py:53
  43.9 0.0 all-gather.7.cloned.1.call-start
  43.9 0.0 copy-done.5
  44.0 7.7 %all-to-all-done = bf16[8,2,8192]{2,1,0:T(2,128)(2,1)S(1)} async-done(((bf16[8,2,8192]{2,1,0:T(2,128)(2,1)}), bf16[8,2,8192]{2,1,0:T(2,128)(2,1)S(1)}, u32[]{:S(2)}, u32[]{:S(2)}) %all-to-all-start) | async-done | bytes 262176 | tf_op jit(solution)/shard_map/all_to_all | solution.py:53
  51.7 0.3 reshape.178
  52.0 0.4 add_convert_fusion
  52.4 11.8 %all_to_all.8 = bf16[8,32,512]{2,1,0:T(8,128)(2,1)S(1)} all-to-all(bf16[8,32,512]{2,1,0:T(8,128)(2,1)S(1)} %add_convert_fusion), channel_id=1, replica_groups=mesh['snap'=8,'vert'=4] {'snap'}, dimensions={0} | all-to-all | bytes 524288 | tf_op jit(solution)/shard_map/all_to_all | solution.py:65
  64.2 0.0 copy-done.4
  64.2 1.0 %convolution_convert_fusion = bf16[256,512]{1,0:T(8,128)(2,1)} fusion(bf16[256,512]{1,0:T(8,128)(2,1)S(1)} %bitcast.69, bf16[512,512]{1,0:T(8,128)(2,1)S(1)} %copy-done.4), kind=kOutput, calls=%fused_computation.17 | convolution fusion | flops 134348800 | bytes 1048576 | tf_op jit(solution)/shard_map/svf,fg->svg/dot_general | solution.py:32
  65.2 0.0 all-gather.7.cloned.1.call-update
  65.2 17.2 %all-gather.7.cloned.1.call-done = bf16[1024,512]{1,0:T(8,128)(2,1)} async-done(((bf16[256,512]{1,0:T(8,128)(2,1)}), bf16[1024,512]{1,0:T(8,128)(2,1)}) %all-gather.7.cloned.1.call-update) | async-done | bytes 1048592 | tf_op jit(solution)/shard_map/all_gather | solution.py:19
  82.5 0.0 copy-done.6
  82.5 0.0 copy-start.3
  82.5 2.6 %fusion.8 = bf16[2,12,128,512]{3,1,2,0:T(8,128)(2,1)S(1)} fusion(bf16[8,128,512,1]{2,1,0,3:T(8,128)(2,1)} %bitcast.75, s32[2,12]{1,0:T(2,128)S(1)} %bitcast.95, pred[2,12]{1,0:T(4,128)(4,1)S(1)} %iota_compare_fusion.1), kind=kOutput, calls=%fused_computation.21 | convolution fusion | flops 25166592 | bytes 4194424 | tf_op jit(solution)/shard_map/srkp,sptf->srktf/dot_general | solution.py:22
  85.0 3.5 %fusion.1 = f32[2,512,128,1]{1,2,3,0:T(8,128)S(1)} fusion(bf16[2,12,128,512]{3,1,2,0:T(8,128)(2,1)S(1)} %fusion.8, bf16[1,2,12,128,128]{4,3,2,1,0:T(8,128)(2,1)S(1)} %copy-done), kind=kOutput, calls=%fused_computation.10 | convolution fusion | flops 402653184 | bytes 4456448 | tf_op jit(solution)/shard_map/srkij,srkjf->srif/dot_general | solution.py:25
  88.5 0.0 copy-done.3
  88.5 1.0 %fusion.6 = bf16[1,256,512]{2,1,0:T(8,128)(2,1)} fusion(f32[256,512]{1,0:T(8,128)S(1)} %bitcast.76, bf16[256,512]{1,0:T(8,128)(2,1)S(1)} %bitcast.70, bf16[512,512]{1,0:T(8,128)(2,1)S(1)} %copy-done.3), kind=kOutput, calls=%fused_computation.19 | convolution fusion | flops 134610944 | bytes 1572864 | tf_op jit(solution)/shard_map/svf,fg->svg/dot_general | solution.py:36
  (2 shorter events, 0.1 us)
Async XLA Ops:
  6.5 24.2 %copy-start = (bf16[1,2,12,128,128]{4,3,2,1,0:T(8,128)(2,1)S(1)}, bf16[1,2,12,128,128]{4,3,2,1,0:T(8,128)(2,1)}, u32[]{:S(2)}) copy-start(bf16[1,2,12,128,128]{4,3,2,1,0:T(8,128)(2,1)} %param.10) | copy-start | bytes 2359300
  6.5 21.6 %all-gather.5.cloned.1.call-start = ((), (), s32[]{:S(2)}) async-start(), calls=%async_computation.2 | async-start | bytes 1310720 | tf_op jit(solution)/shard_map/all_gather | solution.py:19
  28.2 6.2 %copy-start.1 = (bf16[1,256,512]{2,1,0:T(8,128)(2,1)S(1)}, bf16[1,256,512]{2,1,0:T(8,128)(2,1)}, u32[]{:S(2)}) copy-start(bf16[1,256,512]{2,1,0:T(8,128)(2,1)} %param.9) | copy-start | bytes 786436
  28.2 6.2 %copy-start.2 = (bf16[512,512]{1,0:T(8,128)(2,1)S(1)}, bf16[512,512]{1,0:T(8,128)(2,1)}, u32[]{:S(2)}) copy-start(bf16[512,512]{1,0:T(8,128)(2,1)} %param.14) | copy-start | bytes 1572868
  30.8 13.2 %copy-start.5 = (f32[16,512]{1,0:T(8,128)S(1)}, f32[16,512]{1,0:T(8,128)}, u32[]{:S(2)}) copy-start(f32[16,512]{1,0:T(8,128)} %param.15) | copy-start | bytes 98308
  34.3 29.9 %copy-start.4 = (bf16[512,512]{1,0:T(8,128)(2,1)S(1)}, bf16[512,512]{1,0:T(8,128)(2,1)}, u32[]{:S(2)}) copy-start(bf16[512,512]{1,0:T(8,128)(2,1)} %param.16) | copy-start | bytes 1572868
  34.3 48.1 %copy-start.6 = (s32[1,2,12]{2,1,0:T(2,128)S(1)}, s32[1,2,12]{2,1,0:T(2,128)}, u32[]{:S(2)}) copy-start(s32[1,2,12]{2,1,0:T(2,128)} %param.11) | copy-start | bytes 292
  38.7 13.0 %all-to-all-start = ((bf16[8,2,8192]{2,1,0:T(2,128)(2,1)}), bf16[8,2,8192]{2,1,0:T(2,128)(2,1)S(1)}, u32[]{:S(2)}, u32[]{:S(2)}) async-start(bf16[8,2,8192]{2,1,0:T(2,128)(2,1)} %reshape.177), calls=%async_computation | async-start | bytes 524288 | tf_op jit(solution)/shard_map/all_to_all | solution.py:53
  43.9 38.6 %all-gather.7.cloned.1.call-start = ((), (), s32[]{:S(2)}) async-start(), calls=%async_computation.3 | async-start | bytes 1310720 | tf_op jit(solution)/shard_map/all_gather | solution.py:19
  82.5 6.1 %copy-start.3 = (bf16[512,512]{1,0:T(8,128)(2,1)S(1)}, bf16[512,512]{1,0:T(8,128)(2,1)}, u32[]{:S(2)}) copy-start(bf16[512,512]{1,0:T(8,128)(2,1)} %param.17) | copy-start | bytes 1572868
Sparse Core Ops, SparseCore 0:
  8.9 19.1 all-gather.4
  65.3 17.0 all-gather.6
where the time goes:
time: 97 us; the launch traced here: 96.4 us
  waiting for transfers between devices  43.7 us (45%)
  matrix products  16.7 us (17%)
  between operations  13.5 us (14%)
  blocking collectives  11.8 us (12%)
  starting transfers between devices  5.27 us (5%)
  other arithmetic  3.35 us (3%)
  local copies, waits for them, and re-layouts  2.14 us (2%)
    all_gather x2, waiting for transfers between devices, aggregate(): piece = lax.all_gather(messages, 'vert', axis=1, tiled=True)  35.9 us
    all_to_all x1, blocking collectives, shards(): lax.all_to_all(mixed, 'snap', split_axis=0, concat_axis=1, tiled=True)  11.8 us
    all_to_all x1, waiting for transfers between devices, shards(): lax.all_to_all(hidden, 'snap', split_axis=1, concat_axis=0, tiled=True)  7.72 us
    dot_general x2, matrix products, aggregate(): jnp.einsum('srkij,srkjf->srif', tile_values, chosen, preferred_element_ty...  6.97 us
    all_to_all x1, starting transfers between devices, shards(): lax.all_to_all(hidden, 'snap', split_axis=1, concat_axis=0, tiled=True)  5.23 us
    dot_general x2, matrix products, aggregate(): jnp.einsum('srkp,sptf->srktf', table, blocks, preferred_element_type=jnp....  5.19 us
    dot_general x2, matrix products, graph_layer(): jnp.einsum('svf,fg->svg', inputs, w_message, preferred_element_type=jnp.f...  3.2 us
    unnamed x1, other arithmetic  2.21 us
  transfers between devices with their start and end apart: 3, of which 3 were waited for; matrix products, arithmetic and copies ran while one was open for 1% of the time, Pallas kernels for 0%

commit v1 on v0

v1 whole, which is shorter than its diff:
```python
import functools

import jax
import jax.numpy as jnp
from jax import lax
from jax.experimental import pallas as pl
from jax.experimental.pallas import tpu as pltpu
from jax.sharding import PartitionSpec as P

MESH = pl.DeviceIdType.MESH
HALVES = 2
GROUPS = 2
CHUNKS = 4
F32 = jnp.float32
BF16 = jnp.bfloat16


def flip(index, mask):
    out, bit = index, 1
    while bit <= mask:
        if mask & bit:
            out = out + (1 - 2 * ((index // bit) % 2)) * bit
        bit *= 2
    return out


def kernel(
    sizes,
    features,
    tile_values,
    columns,
    counts,
    message_one,
    root_one,
    time_taps,
    message_two,
    root_two,
    out,
    feats,
    tiles,
    dense,
    weights,
    taps,
    acc,
    total,
    hid,
    by_time,
    mix,
    mixed,
    local_sem,
    near_sem,
    y1_send,
    y1_recv,
    f1_send,
    f1_recv,
    p2_send,
    p2_recv,
    p3_send,
    p3_recv,
    y4_send,
    y4_recv,
    s4_send,
    s4_recv,
    f4_send,
    f4_recv,
):
    n, nv, rows, width, slots, tile = sizes
    ny = nv // 2
    per = rows // tile
    cols = width // HALVES
    piece_rows = max(rows // n, 16)
    across = n // (rows // piece_rows)
    piece_cols = cols // across
    me_s, me_v = lax.axis_index("snap"), lax.axis_index("vert")
    y, core = me_v // 2, me_v % 2
    sib = y * 2 + 1 - core

    def piece(p):
        r = pl.multiple_of((p // across) * piece_rows, piece_rows)
        if across == 1:
            return pl.ds(r, piece_rows), slice(0, piece_cols)
        return pl.ds(r, piece_rows), pl.ds(pl.multiple_of((p % across) * piece_cols, piece_cols), piece_cols)

    def remote(src, dst, send, recv, s, v):
        return pltpu.make_async_remote_copy(
            src_ref=src, dst_ref=dst, send_sem=send, recv_sem=recv, device_id=(s, v), device_id_type=MESH
        )

    sent = []

    def go(*args):
        copy = remote(*args)
        copy.start()
        sent.append(copy)

    def y_to(d):
        return ((y + d) % ny) * 2 + core

    def y_from(d):
        return ((y - d + ny) % ny) * 2 + core

    own_feats = pltpu.make_async_copy(features.at[0], feats.at[me_v], local_sem.at[0])
    load_tiles = pltpu.make_async_copy(tile_values.at[0], tiles, local_sem.at[1])
    loads = [
        pltpu.make_async_copy(ref, weights.at[i], local_sem.at[2 + i])
        for i, ref in enumerate((root_one, message_one, root_two, message_two))
    ]
    load_taps = pltpu.make_async_copy(time_taps, taps, local_sem.at[6])
    load_tiles.start()
    own_feats.start()
    for load in loads:
        load.start()
    load_taps.start()

    barrier = pltpu.get_barrier_semaphore()
    for d in range(1, n):
        pl.semaphore_signal(barrier, inc=1, device_id=(flip(me_s, d), me_v), device_id_type=MESH)
    for d in range(1, ny):
        pl.semaphore_signal(barrier, inc=1, device_id=(me_s, y_to(d)), device_id_type=MESH)
    pl.semaphore_signal(barrier, inc=1, device_id=(me_s, sib), device_id_type=MESH)
    pl.semaphore_wait(barrier, n - 1 + ny)

    step = rows // CHUNKS
    for q in range(CHUNKS):
        part = pl.ds(q * step, step)
        for d in range(1, ny):
            go(features.at[0, part], feats.at[me_v, part], y1_send.at[d, q], y1_recv.at[d, q], me_s, y_to(d))
    go(features.at[0], feats.at[me_v], near_sem.at[0], near_sem.at[1], me_s, sib)

    def pass_on(q):
        part = pl.ds(q * step, step)
        for d in range(1, ny):
            src = y_from(d)
            block = feats.at[src, part]
            remote(block, block, y1_send.at[d, q], y1_recv.at[d, q], me_s, src).wait_recv()
            go(block, block, f1_send.at[d, q], f1_recv.at[d, q], me_s, sib)

    load_tiles.wait()
    live = [
        [jnp.where(k < counts[0, b], columns[0, b, k], -1) for k in range(slots)] for b in range(per)
    ]

    def fill(v, carry):
        for b in range(per):
            for j in range(per):
                block = jnp.zeros((tile, tile), F32)
                for k in range(slots):
                    scale = jnp.where(live[b][k] == v * per + j, 1.0, 0.0).astype(F32)
                    block = block + scale * tiles[b, k].astype(F32)
                dense[v, b * tile : (b + 1) * tile, j * tile : (j + 1) * tile] = block.astype(BF16)
        return carry

    lax.fori_loop(0, nv, fill, 0)

    def dot(a, b):
        return jnp.dot(a, b, preferred_element_type=F32)

    pass_on(0)
    own_feats.wait()
    loads[0].wait()
    total[...] = dot(feats[me_v], weights[0])
    pass_on(1)
    acc[...] = dot(dense[me_v], feats[me_v])
    for q in range(2, CHUNKS):
        pass_on(q)
    block = feats.at[sib]
    remote(block, block, near_sem.at[0], near_sem.at[1], me_s, sib).wait_recv()
    acc[...] += dot(dense[sib], feats[sib])
    for d in range(1, ny):
        src = y_from(d)
        acc[...] += dot(dense[src], feats[src])
    for d in range(1, ny):
        src = ((y - d + ny) % ny) * 2 + 1 - core
        for q in range(CHUNKS):
            block = feats.at[src, pl.ds(q * step, step)]
            remote(block, block, f1_send.at[d, q], f1_recv.at[d, q], me_s, sib).wait_recv()
        acc[...] += dot(dense[src], feats[src])

    loads[1].wait()
    order = list(range(n // 2, n)) + list(range(1, n // 2))
    near = acc[...].astype(BF16)
    for h in range(HALVES):
        lanes = slice(h * cols, (h + 1) * cols)
        value = total[:, lanes] + dot(near, weights[1, :, lanes])
        hid[h] = jnp.maximum(value, 0.0).astype(BF16)
        for d in order:
            p = flip(me_s, d)
            r, c = piece(p)
            go(hid.at[h, r, c], by_time.at[h, me_s], p2_send.at[h, d], p2_recv.at[h, d], p, me_v)

    load_taps.wait()
    for h in range(HALVES):
        r, c = piece(me_s)
        by_time[h, me_s] = hid[h, r, c]
        for d in range(1, n):
            p = flip(me_s, d)
            block = by_time.at[h, p]
            remote(block, block, p2_send.at[h, d], p2_recv.at[h, d], p, me_v).wait_recv()
        shift = 0 if across == 1 else (me_s % across) * piece_cols
        for i in range(0, piece_rows, 16):
            for j in range(0, piece_cols, 128):
                at = h * cols + j + shift
                if across > 1:
                    at = pl.multiple_of(at, 128)
                filt = taps[:, pl.ds(at, 128)]
                wide = [by_time[h, t, i : i + 16, j : j + 128].astype(F32) for t in range(n)]
                for t in range(n):
                    value = filt[0:1] * wide[t]
                    for k in range(1, min(filt.shape[0] - 1, t) + 1):
                        value = value + filt[k : k + 1] * wide[t - k]
                    mix[h, t, i : i + 16, j : j + 128] = value.astype(BF16)
        for d in order:
            p = flip(me_s, d)
            go(mix.at[h, p], mixed.at[h, me_v, r, c], p3_send.at[h, d], p3_recv.at[h, d], p, me_v)
        mixed[h, me_v, r, c] = mix[h, me_s]

    half = rows // GROUPS
    size = n // GROUPS

    def group_rows(g):
        start = me_s // size if g == 0 else 1 - me_s // size
        return pl.ds(pl.multiple_of(start * half, half), half)

    def send_group(h, g):
        for d in range(g * size, (g + 1) * size):
            if d > 0:
                p = flip(me_s, d)
                r, c = piece(p)
                block = mixed.at[h, me_v, r, c]
                remote(block, block, p3_send.at[h, d], p3_recv.at[h, d], p, me_v).wait_recv()
        block = mixed.at[h, me_v, group_rows(g)]
        for d in range(1, ny):
            go(block, block, y4_send.at[d, h, g], y4_recv.at[d, h, g], me_s, y_to(d))
        go(block, block, s4_send.at[h, g], s4_recv.at[h, g], me_s, sib)

    def pass_group(h, g):
        for d in range(1, ny):
            src = y_from(d)
            block = mixed.at[h, src, group_rows(g)]
            remote(block, block, y4_send.at[d, h, g], y4_recv.at[d, h, g], me_s, src).wait_recv()
            go(block, block, f4_send.at[d, h, g], f4_recv.at[d, h, g], me_s, sib)

    def near_part(h):
        lanes = slice(h * cols, (h + 1) * cols)
        acc[:, lanes] = dot(dense[me_v], mixed[h, me_v])
        for g in range(GROUPS):
            block = mixed.at[h, sib, group_rows(g)]
            remote(block, block, s4_send.at[h, g], s4_recv.at[h, g], me_s, sib).wait_recv()
        acc[:, lanes] += dot(dense[sib], mixed[h, sib])
        own = dot(mixed[h, me_v], weights[2, lanes, :])
        if h == 0:
            total[...] = own
        else:
            total[...] += own

    def far_part(h):
        lanes = slice(h * cols, (h + 1) * cols)
        for d in range(1, ny):
            src = y_from(d)
            acc[:, lanes] += dot(dense[src], mixed[h, src])
        for d in range(1, ny):
            src = ((y - d + ny) % ny) * 2 + 1 - core
            for g in range(GROUPS):
                block = mixed.at[h, src, group_rows(g)]
                remote(block, block, f4_send.at[d, h, g], f4_recv.at[d, h, g], me_s, sib).wait_recv()
            acc[:, lanes] += dot(dense[src], mixed[h, src])
        total[...] += dot(acc[:, lanes].astype(BF16), weights[3, lanes, :])

    loads[2].wait()
    loads[3].wait()
    send_group(0, 0)
    send_group(0, 1)
    pass_group(0, 0)
    send_group(1, 0)
    pass_group(0, 1)
    near_part(0)
    send_group(1, 1)
    pass_group(1, 0)
    far_part(0)
    pass_group(1, 1)
    near_part(1)
    far_part(1)
    out[0] = jnp.maximum(total[...], 0.0).astype(BF16)
    for copy in sent:
        copy.wait_send()


def shards(n, nv, features, tile_values, tile_column, tile_count, *rest):
    _, rows, width = features.shape
    _, per, slots, tile, _ = tile_values.shape
    ny = nv // 2
    cols = width // HALVES
    piece_rows = max(rows // n, 16)
    piece_cols = cols // (n // (rows // piece_rows))
    taps = rest[2].shape[0]
    dma = pltpu.SemaphoreType.DMA
    hbm = pl.BlockSpec(memory_space=pl.ANY)
    smem = pl.BlockSpec(memory_space=pltpu.SMEM)
    return pl.pallas_call(
        functools.partial(kernel, (n, nv, rows, width, slots, tile)),
        out_shape=jax.ShapeDtypeStruct((1, rows, width), BF16),
        in_specs=[hbm, hbm, smem, smem] + [hbm] * 5,
        out_specs=pl.BlockSpec(memory_space=pltpu.VMEM),
        scratch_shapes=[
            pltpu.VMEM((nv, rows, width), BF16),
            pltpu.VMEM((per, slots, tile, tile), BF16),
            pltpu.VMEM((nv, rows, rows), BF16),
            pltpu.VMEM((4, width, width), BF16),
            pltpu.VMEM((taps, width), F32),
            pltpu.VMEM((rows, width), F32),
            pltpu.VMEM((rows, width), F32),
            pltpu.VMEM((HALVES, rows, cols), BF16),
            pltpu.VMEM((HALVES, n, piece_rows, piece_cols), BF16),
            pltpu.VMEM((HALVES, n, piece_rows, piece_cols), BF16),
            pltpu.VMEM((HALVES, nv, rows, cols), BF16),
            dma((7,)),
            dma((2,)),
            dma((ny, CHUNKS)),
            dma((ny, CHUNKS)),
            dma((ny, CHUNKS)),
            dma((ny, CHUNKS)),
            dma((HALVES, n)),
            dma((HALVES, n)),
            dma((HALVES, n)),
            dma((HALVES, n)),
            dma((ny, HALVES, GROUPS)),
            dma((ny, HALVES, GROUPS)),
            dma((HALVES, GROUPS)),
            dma((HALVES, GROUPS)),
            dma((ny, HALVES, GROUPS)),
            dma((ny, HALVES, GROUPS)),
        ],
        compiler_params=pltpu.CompilerParams(
            collective_id=0, has_side_effects=True, vmem_limit_bytes=40 * 1024 * 1024
        ),
    )(features, tile_values, tile_column, tile_count, *rest)


def solution(mesh):
    n, nv = mesh.shape["snap"], mesh.shape["vert"]
    return jax.shard_map(
        functools.partial(shards, n, nv),
        mesh=mesh,
        in_specs=(
            P("snap", "vert", None),
            P("snap", "vert", None, None, None),
            P("snap", "vert", None),
            P("snap", "vert"),
            P(),
            P(),
            P(),
            P(),
            P(),
        ),
        out_specs=P("snap", "vert", None),
        check_vma=False,
    )
```

time: 97 us -> 46.2 us (0.48)
  waiting for transfers between devices: 43.7 us -> 0 us
  Pallas kernels: 0 us -> 36.7 us
  matrix products: 16.7 us -> 0 us
  between operations: 13.5 us -> 0.02 us
  blocking collectives: 11.8 us -> 0 us
  local copies, waits for them, and re-layouts: 2.14 us -> 9.04 us
  starting transfers between devices: 5.27 us -> 0 us
  other arithmetic: 3.35 us -> 0 us
    pallas_call x0 -> x1, Pallas kernels: none -> 36.7 us  [shards(): pl.pallas_call(functools.partial(kernel, (n, nv, rows, width, slots, tile...]
    all_gather x2 -> x0, waiting for transfers between devices: 35.9 us -> none  [aggregate(): piece = lax.all_gather(messages, 'vert', axis=1, tiled=True)]
    dot_general x8 -> x0, matrix products: 16.7 us -> none  [the longest x2 6.97 us: aggregate(): jnp.einsum('srkij,srkjf->srif', tile_values, chosen, preferred_element_ty...]
    all_to_all x1 -> x0, blocking collectives: 11.8 us -> none  [shards(): lax.all_to_all(mixed, 'snap', split_axis=0, concat_axis=1, tiled=True)]
    all_to_all x1 -> x0, waiting for transfers between devices: 7.72 us -> none  [shards(): lax.all_to_all(hidden, 'snap', split_axis=1, concat_axis=0, tiled=True)]
    unnamed x18 -> x19, local copies, waits for them, and re-layouts: 1.73 us -> 9.04 us
    all_to_all x1 -> x0, starting transfers between devices: 5.23 us -> none  [shards(): lax.all_to_all(hidden, 'snap', split_axis=1, concat_axis=0, tiled=True)]
    unnamed x1 -> x0, other arithmetic: 2.21 us -> none
  transfers between devices with their start and end apart: 3 -> 0, of which waited for: 3 -> 0; matrix products, arithmetic and copies ran while one was open for 1% -> 0% of each run, Pallas kernels for 0% -> 0%
where the time goes in v1:
time: 46.2 us; the launch traced here: 45.7 us
  Pallas kernels  36.7 us (79%)
  local copies, waits for them, and re-layouts  9.04 us (20%)
    pallas_call x1, Pallas kernels, shards(): pl.pallas_call(functools.partial(kernel, (n, nv, rows, width, slots, tile...  36.7 us
    unnamed x19, local copies, waits for them, and re-layouts  9.04 us

profile of v1, /device:TPU:1, one launch (start us, length us, event | category | flops | bytes accessed | tf_op | source)
XLA Modules:
  0.0 45.7 jit_solution(13000775763705109120)
XLA Ops:
  0.0 0.0 copy-start
  0.0 1.1 %copy-done = bf16[1,2,12,128,128]{4,3,2,1,0:T(8,128)(2,1)S(1)} copy-done((bf16[1,2,12,128,128]{4,3,2,1,0:T(8,128)(2,1)S(1)}, bf16[1,2,12,128,128]{4,3,2,1,0:T(8,128)(2,1)}, u32[]{:S(2)}) %copy-start) | copy-done | bytes 786456
  1.1 0.0 copy-start.1
  1.1 1.0 %copy-done.1 = bf16[512,512]{1,0:T(8,128)(2,1)S(1)} copy-done((bf16[512,512]{1,0:T(8,128)(2,1)S(1)}, bf16[512,512]{1,0:T(8,128)(2,1)}, u32[]{:S(2)}) %copy-start.1) | copy-done | bytes 524312
  2.2 0.0 copy-start.2
  2.2 1.0 %copy-done.2 = bf16[512,512]{1,0:T(8,128)(2,1)S(1)} copy-done((bf16[512,512]{1,0:T(8,128)(2,1)S(1)}, bf16[512,512]{1,0:T(8,128)(2,1)}, u32[]{:S(2)}) %copy-start.2) | copy-done | bytes 524312
  3.2 0.0 copy-start.3
  3.2 1.0 %copy-done.3 = bf16[512,512]{1,0:T(8,128)(2,1)S(1)} copy-done((bf16[512,512]{1,0:T(8,128)(2,1)S(1)}, bf16[512,512]{1,0:T(8,128)(2,1)}, u32[]{:S(2)}) %copy-start.3) | copy-done | bytes 524312
  4.3 0.0 copy-start.4
  4.3 1.0 %copy-done.4 = bf16[512,512]{1,0:T(8,128)(2,1)S(1)} copy-done((bf16[512,512]{1,0:T(8,128)(2,1)S(1)}, bf16[512,512]{1,0:T(8,128)(2,1)}, u32[]{:S(2)}) %copy-start.4) | copy-done | bytes 524312
  5.3 0.0 copy-start.5
  5.3 0.9 %copy-done.5 = bf16[1,256,512]{2,1,0:T(8,128)(2,1)S(1)} copy-done((bf16[1,256,512]{2,1,0:T(8,128)(2,1)S(1)}, bf16[1,256,512]{2,1,0:T(8,128)(2,1)}, u32[]{:S(2)}) %copy-start.5) | copy-done | bytes 262168
  6.3 0.0 copy-start.6
  6.3 0.8 %copy-done.6 = f32[16,512]{1,0:T(8,128)S(1)} copy-done((f32[16,512]{1,0:T(8,128)S(1)}, f32[16,512]{1,0:T(8,128)}, u32[]{:S(2)}) %copy-start.6) | copy-done | bytes 32792
  7.0 0.0 copy-start.7
  7.0 0.7 %copy-done.7 = s32[1,2,12]{2,1,0:T(2,128)S(1)} copy-done((s32[1,2,12]{2,1,0:T(2,128)S(1)}, s32[1,2,12]{2,1,0:T(2,128)}, u32[]{:S(2)}) %copy-start.7) | copy-done | bytes 120
  7.7 0.0 copy-start.8
  7.7 0.7 %copy-done.8 = s32[1,2]{1,0:T(1,128)S(1)} copy-done((s32[1,2]{1,0:T(1,128)S(1)}, s32[1,2]{1,0:T(1,128)}, u32[]{:S(2)}) %copy-start.8) | copy-done | bytes 32
  8.3 36.7 %shard_map.91 = bf16[1,256,512]{2,1,0:T(8,128)(2,1)S(1)} custom-call(bf16[1,256,512]{2,1,0:T(8,128)(2,1)S(1)} %copy-done.5, bf16[1,2,12,128,128]{4,3,2,1,0:T(8,128)(2,1)S(1)} %copy-done, s32[1,2,12]{2,1,0:T(2,128)S(1)} %copy-done.7, s32[1,2]{1,0:T(1,128)S(1)} %copy-done.8, bf16[512,512]{1,0:T(8,128)(2,1)S(1)} %copy-done.1, bf16[512,512]{1,0:T(8,128)(2,1)S(1)} %copy-done.2, ...), custom_call_target="tpu_custom_call" | custom-call | tf_op jit(solution)/shard_map/pallas_call | solution.py:299
  45.0 0.7 %copy.11 = bf16[1,256,512]{2,1,0:T(8,128)(2,1)} copy(bf16[1,256,512]{2,1,0:T(8,128)(2,1)S(1)} %shard_map.91) | data formatting | bytes 524288
Async XLA Ops:
  0.0 1.1 %copy-start = (bf16[1,2,12,128,128]{4,3,2,1,0:T(8,128)(2,1)S(1)}, bf16[1,2,12,128,128]{4,3,2,1,0:T(8,128)(2,1)}, u32[]{:S(2)}) copy-start(bf16[1,2,12,128,128]{4,3,2,1,0:T(8,128)(2,1)} %tile_values.1) | copy-start | bytes 2359300
  1.1 1.0 %copy-start.1 = (bf16[512,512]{1,0:T(8,128)(2,1)S(1)}, bf16[512,512]{1,0:T(8,128)(2,1)}, u32[]{:S(2)}) copy-start(bf16[512,512]{1,0:T(8,128)(2,1)} %message_one.1) | copy-start | bytes 1572868
  2.2 1.0 %copy-start.2 = (bf16[512,512]{1,0:T(8,128)(2,1)S(1)}, bf16[512,512]{1,0:T(8,128)(2,1)}, u32[]{:S(2)}) copy-start(bf16[512,512]{1,0:T(8,128)(2,1)} %root_one.1) | copy-start | bytes 1572868
  3.2 1.0 %copy-start.3 = (bf16[512,512]{1,0:T(8,128)(2,1)S(1)}, bf16[512,512]{1,0:T(8,128)(2,1)}, u32[]{:S(2)}) copy-start(bf16[512,512]{1,0:T(8,128)(2,1)} %message_two.1) | copy-start | bytes 1572868
  4.3 1.0 %copy-start.4 = (bf16[512,512]{1,0:T(8,128)(2,1)S(1)}, bf16[512,512]{1,0:T(8,128)(2,1)}, u32[]{:S(2)}) copy-start(bf16[512,512]{1,0:T(8,128)(2,1)} %root_two.1) | copy-start | bytes 1572868
  5.3 0.9 %copy-start.5 = (bf16[1,256,512]{2,1,0:T(8,128)(2,1)S(1)}, bf16[1,256,512]{2,1,0:T(8,128)(2,1)}, u32[]{:S(2)}) copy-start(bf16[1,256,512]{2,1,0:T(8,128)(2,1)} %features.1) | copy-start | bytes 786436
  6.3 0.8 %copy-start.6 = (f32[16,512]{1,0:T(8,128)S(1)}, f32[16,512]{1,0:T(8,128)}, u32[]{:S(2)}) copy-start(f32[16,512]{1,0:T(8,128)} %time_taps.1) | copy-start | bytes 98308
  7.0 0.7 %copy-start.7 = (s32[1,2,12]{2,1,0:T(2,128)S(1)}, s32[1,2,12]{2,1,0:T(2,128)}, u32[]{:S(2)}) copy-start(s32[1,2,12]{2,1,0:T(2,128)} %columns.1) | copy-start | bytes 292
  7.7 0.7 %copy-start.8 = (s32[1,2]{1,0:T(1,128)S(1)}, s32[1,2]{1,0:T(1,128)}, u32[]{:S(2)}) copy-start(s32[1,2]{1,0:T(1,128)} %counts.1) | copy-start | bytes 28

commit v2 on v1

--- a/solution.py
+++ b/solution.py
@@ -36,6 +36,8 @@
     message_two,
     root_two,
     out,
+    column_smem,
+    count_smem,
     feats,
     tiles,
     dense,
@@ -106,6 +108,10 @@
         for i, ref in enumerate((root_one, message_one, root_two, message_two))
     ]
     load_taps = pltpu.make_async_copy(time_taps, taps, local_sem.at[6])
+    load_columns = pltpu.make_async_copy(columns.at[0], column_smem, local_sem.at[7])
+    load_counts = pltpu.make_async_copy(counts, count_smem, local_sem.at[8])
+    load_columns.start()
+    load_counts.start()
     load_tiles.start()
     own_feats.start()
     for load in loads:
@@ -135,9 +141,11 @@
             remote(block, block, y1_send.at[d, q], y1_recv.at[d, q], me_s, src).wait_recv()
             go(block, block, f1_send.at[d, q], f1_recv.at[d, q], me_s, sib)
 
+    load_columns.wait()
+    load_counts.wait()
     load_tiles.wait()
     live = [
-        [jnp.where(k < counts[0, b], columns[0, b, k], -1) for k in range(slots)] for b in range(per)
+        [jnp.where(k < count_smem[0, b], column_smem[b, k], -1) for k in range(slots)] for b in range(per)
     ]
 
     def fill(v, carry):
@@ -294,14 +302,15 @@
     piece_cols = cols // (n // (rows // piece_rows))
     taps = rest[2].shape[0]
     dma = pltpu.SemaphoreType.DMA
-    hbm = pl.BlockSpec(memory_space=pl.ANY)
-    smem = pl.BlockSpec(memory_space=pltpu.SMEM)
+    hbm = pl.BlockSpec(memory_space=pltpu.HBM)
     return pl.pallas_call(
         functools.partial(kernel, (n, nv, rows, width, slots, tile)),
         out_shape=jax.ShapeDtypeStruct((1, rows, width), BF16),
-        in_specs=[hbm, hbm, smem, smem] + [hbm] * 5,
+        in_specs=[hbm] * 9,
         out_specs=pl.BlockSpec(memory_space=pltpu.VMEM),
         scratch_shapes=[
+            pltpu.SMEM((per, slots), jnp.int32),
+            pltpu.SMEM((1, per), jnp.int32),
             pltpu.VMEM((nv, rows, width), BF16),
             pltpu.VMEM((per, slots, tile, tile), BF16),
             pltpu.VMEM((nv, rows, rows), BF16),
@@ -313,7 +322,7 @@
             pltpu.VMEM((HALVES, n, piece_rows, piece_cols), BF16),
             pltpu.VMEM((HALVES, n, piece_rows, piece_cols), BF16),
             pltpu.VMEM((HALVES, nv, rows, cols), BF16),
-            dma((7,)),
+            dma((9,)),
             dma((2,)),
             dma((ny, CHUNKS)),
             dma((ny, CHUNKS)),
@@ -331,7 +340,7 @@
             dma((ny, HALVES, GROUPS)),
         ],
         compiler_params=pltpu.CompilerParams(
-            collective_id=0, has_side_effects=True, vmem_limit_bytes=40 * 1024 * 1024
+            collective_id=0, has_side_effects=True, vmem_limit_bytes=64 * 1024 * 1024
         ),
     )(features, tile_values, tile_column, tile_count, *rest)
 

time: 46.2 us -> 38.6 us (0.84)
  local copies, waits for them, and re-layouts: 9.04 us -> 1.67 us
    unnamed x19 -> x1, local copies, waits for them, and re-layouts: 9.04 us -> 1.67 us
where the time goes in v2:
time: 38.6 us; the launch traced here: 38.4 us
  Pallas kernels  36.8 us (95%)
  local copies, waits for them, and re-layouts  1.67 us (4%)
    pallas_call x1, Pallas kernels, shards(): pl.pallas_call(functools.partial(kernel, (n, nv, rows, width, slots, tile...  36.8 us
    unnamed x1, local copies, waits for them, and re-layouts  1.67 us

profile of v2, /device:TPU:1, one launch (start us, length us, event | category | flops | bytes accessed | tf_op | source)
XLA Modules:
  0.0 38.4 jit_solution(17323023491736282676)
XLA Ops:
  0.0 36.8 %shard_map.91 = bf16[1,256,512]{2,1,0:T(8,128)(2,1)} custom-call(bf16[1,256,512]{2,1,0:T(8,128)(2,1)} %features.1, bf16[1,2,12,128,128]{4,3,2,1,0:T(8,128)(2,1)} %tile_values.1, s32[1,2,12]{2,1,0:T(2,128)} %columns.1, s32[1,2]{1,0:T(1,128)} %counts.1, bf16[512,512]{1,0:T(8,128)(2,1)} %message_one.1, bf16[512,512]{1,0:T(8,128)(2,1)} %root_one.1, ...), custom_call_target="tpu_custom_call" | custom-call | tf_op jit(solution)/shard_map/pallas_call | solution.py:306
  36.8 1.7 %copy.11 = bf16[1,256,512]{2,1,0:T(8,128)(2,1)} copy(bf16[1,256,512]{2,1,0:T(8,128)(2,1)} %shard_map.91) | data formatting | bytes 524288

commit v3 on v2

--- a/solution.py
+++ b/solution.py
@@ -8,11 +8,17 @@
 from jax.sharding import PartitionSpec as P
 
 MESH = pl.DeviceIdType.MESH
-HALVES = 2
 GROUPS = 2
-CHUNKS = 4
+MOST_PARTS = 4
 F32 = jnp.float32
 BF16 = jnp.bfloat16
+
+
+def cut(n, rows, width):
+    piece_rows = max(rows // n, 16)
+    across = n // (rows // piece_rows)
+    parts = max(1, min(MOST_PARTS, width // 128 // across))
+    return parts, width // parts, across, piece_rows, width // parts // across
 
 
 def flip(index, mask):
@@ -39,6 +45,7 @@
     column_smem,
     count_smem,
     feats,
+    msgs,
     tiles,
     dense,
     weights,
@@ -50,7 +57,8 @@
     mix,
     mixed,
     local_sem,
-    near_sem,
+    near_send,
+    near_recv,
     y1_send,
     y1_recv,
     f1_send,
@@ -69,10 +77,7 @@
     n, nv, rows, width, slots, tile = sizes
     ny = nv // 2
     per = rows // tile
-    cols = width // HALVES
-    piece_rows = max(rows // n, 16)
-    across = n // (rows // piece_rows)
-    piece_cols = cols // across
+    parts, cols, across, piece_rows, piece_cols = cut(n, rows, width)
     me_s, me_v = lax.axis_index("snap"), lax.axis_index("vert")
     y, core = me_v // 2, me_v % 2
     sib = y * 2 + 1 - core
@@ -101,7 +106,7 @@
     def y_from(d):
         return ((y - d + ny) % ny) * 2 + core
 
-    own_feats = pltpu.make_async_copy(features.at[0], feats.at[me_v], local_sem.at[0])
+    load_feats = pltpu.make_async_copy(features.at[0], feats, local_sem.at[0])
     load_tiles = pltpu.make_async_copy(tile_values.at[0], tiles, local_sem.at[1])
     loads = [
         pltpu.make_async_copy(ref, weights.at[i], local_sem.at[2 + i])
@@ -110,13 +115,8 @@
     load_taps = pltpu.make_async_copy(time_taps, taps, local_sem.at[6])
     load_columns = pltpu.make_async_copy(columns.at[0], column_smem, local_sem.at[7])
     load_counts = pltpu.make_async_copy(counts, count_smem, local_sem.at[8])
-    load_columns.start()
-    load_counts.start()
-    load_tiles.start()
-    own_feats.start()
-    for load in loads:
+    for load in (load_feats, loads[1], load_columns, load_counts, load_tiles, loads[0], load_taps, loads[2], loads[3]):
         load.start()
-    load_taps.start()
 
     barrier = pltpu.get_barrier_semaphore()
     for d in range(1, n):
@@ -124,22 +124,30 @@
     for d in range(1, ny):
         pl.semaphore_signal(barrier, inc=1, device_id=(me_s, y_to(d)), device_id_type=MESH)
     pl.semaphore_signal(barrier, inc=1, device_id=(me_s, sib), device_id_type=MESH)
-    pl.semaphore_wait(barrier, n - 1 + ny)
-
-    step = rows // CHUNKS
-    for q in range(CHUNKS):
-        part = pl.ds(q * step, step)
-        for d in range(1, ny):
-            go(features.at[0, part], feats.at[me_v, part], y1_send.at[d, q], y1_recv.at[d, q], me_s, y_to(d))
-    go(features.at[0], feats.at[me_v], near_sem.at[0], near_sem.at[1], me_s, sib)
-
-    def pass_on(q):
-        part = pl.ds(q * step, step)
+
+    def dot(a, b):
+        return jnp.dot(a, b, preferred_element_type=F32)
+
+    def lanes(h):
+        return slice(h * cols, (h + 1) * cols)
+
+    load_feats.wait()
+    loads[1].wait()
+    for h in range(parts):
+        msgs[h, me_v] = dot(feats[...], weights[1, :, lanes(h)]).astype(BF16)
+        if h == 0:
+            pl.semaphore_wait(barrier, n - 1 + ny)
+        block = msgs.at[h, me_v]
+        for d in range(1, ny):
+            go(block, block, y1_send.at[d, h], y1_recv.at[d, h], me_s, y_to(d))
+        go(block, block, near_send.at[h], near_recv.at[h], me_s, sib)
+
+    def pass_on(h):
         for d in range(1, ny):
             src = y_from(d)
-            block = feats.at[src, part]
-            remote(block, block, y1_send.at[d, q], y1_recv.at[d, q], me_s, src).wait_recv()
-            go(block, block, f1_send.at[d, q], f1_recv.at[d, q], me_s, sib)
+            block = msgs.at[h, src]
+            remote(block, block, y1_send.at[d, h], y1_recv.at[d, h], me_s, src).wait_recv()
+            go(block, block, f1_send.at[d, h], f1_recv.at[d, h], me_s, sib)
 
     load_columns.wait()
     load_counts.wait()
@@ -160,44 +168,32 @@
 
     lax.fori_loop(0, nv, fill, 0)
 
-    def dot(a, b):
-        return jnp.dot(a, b, preferred_element_type=F32)
-
-    pass_on(0)
-    own_feats.wait()
+    order = list(range(n // 2, n)) + list(range(1, n // 2))
     loads[0].wait()
-    total[...] = dot(feats[me_v], weights[0])
-    pass_on(1)
-    acc[...] = dot(dense[me_v], feats[me_v])
-    for q in range(2, CHUNKS):
-        pass_on(q)
-    block = feats.at[sib]
-    remote(block, block, near_sem.at[0], near_sem.at[1], me_s, sib).wait_recv()
-    acc[...] += dot(dense[sib], feats[sib])
-    for d in range(1, ny):
-        src = y_from(d)
-        acc[...] += dot(dense[src], feats[src])
-    for d in range(1, ny):
-        src = ((y - d + ny) % ny) * 2 + 1 - core
-        for q in range(CHUNKS):
-            block = feats.at[src, pl.ds(q * step, step)]
-            remote(block, block, f1_send.at[d, q], f1_recv.at[d, q], me_s, sib).wait_recv()
-        acc[...] += dot(dense[src], feats[src])
-
-    loads[1].wait()
-    order = list(range(n // 2, n)) + list(range(1, n // 2))
-    near = acc[...].astype(BF16)
-    for h in range(HALVES):
-        lanes = slice(h * cols, (h + 1) * cols)
-        value = total[:, lanes] + dot(near, weights[1, :, lanes])
+
+    def near_messages(h):
+        total[:, lanes(h)] = dot(feats[...], weights[0, :, lanes(h)])
+        block = msgs.at[h, sib]
+        remote(block, block, near_send.at[h], near_recv.at[h], me_s, sib).wait_recv()
+        total[:, lanes(h)] += dot(dense[me_v], msgs[h, me_v]) + dot(dense[sib], msgs[h, sib])
+
+    def far_messages(h):
+        value = total[:, lanes(h)]
+        for d in range(1, ny):
+            src = y_from(d)
+            value = value + dot(dense[src], msgs[h, src])
+        for d in range(1, ny):
+            src = ((y - d + ny) % ny) * 2 + 1 - core
+            block = msgs.at[h, src]
+            remote(block, block, f1_send.at[d, h], f1_recv.at[d, h], me_s, sib).wait_recv()
+            value = value + dot(dense[src], msgs[h, src])
         hid[h] = jnp.maximum(value, 0.0).astype(BF16)
         for d in order:
             p = flip(me_s, d)
             r, c = piece(p)
             go(hid.at[h, r, c], by_time.at[h, me_s], p2_send.at[h, d], p2_recv.at[h, d], p, me_v)
 
-    load_taps.wait()
-    for h in range(HALVES):
+    def filter_part(h):
         r, c = piece(me_s)
         by_time[h, me_s] = hid[h, r, c]
         for d in range(1, n):
@@ -222,6 +218,20 @@
             go(mix.at[h, p], mixed.at[h, me_v, r, c], p3_send.at[h, d], p3_recv.at[h, d], p, me_v)
         mixed[h, me_v, r, c] = mix[h, me_s]
 
+    pass_on(0)
+    near_messages(0)
+    load_taps.wait()
+    for h in range(parts):
+        if h + 1 < parts:
+            pass_on(h + 1)
+        far_messages(h)
+        if h + 1 < parts:
+            near_messages(h + 1)
+        if h >= 2:
+            filter_part(h - 2)
+    for h in range(max(0, parts - 2), parts):
+        filter_part(h)
+
     half = rows // GROUPS
     size = n // GROUPS
 
@@ -249,46 +259,47 @@
             go(block, block, f4_send.at[d, h, g], f4_recv.at[d, h, g], me_s, sib)
 
     def near_part(h):
-        lanes = slice(h * cols, (h + 1) * cols)
-        acc[:, lanes] = dot(dense[me_v], mixed[h, me_v])
+        value = dot(dense[me_v], mixed[h, me_v])
         for g in range(GROUPS):
             block = mixed.at[h, sib, group_rows(g)]
             remote(block, block, s4_send.at[h, g], s4_recv.at[h, g], me_s, sib).wait_recv()
-        acc[:, lanes] += dot(dense[sib], mixed[h, sib])
-        own = dot(mixed[h, me_v], weights[2, lanes, :])
+        acc[:, lanes(h)] = value + dot(dense[sib], mixed[h, sib])
+        own = dot(mixed[h, me_v], weights[2, lanes(h), :])
         if h == 0:
             total[...] = own
         else:
             total[...] += own
 
     def far_part(h):
-        lanes = slice(h * cols, (h + 1) * cols)
+        value = acc[:, lanes(h)]
         for d in range(1, ny):
             src = y_from(d)
-            acc[:, lanes] += dot(dense[src], mixed[h, src])
+            value = value + dot(dense[src], mixed[h, src])
         for d in range(1, ny):
             src = ((y - d + ny) % ny) * 2 + 1 - core
             for g in range(GROUPS):
                 block = mixed.at[h, src, group_rows(g)]
                 remote(block, block, f4_send.at[d, h, g], f4_recv.at[d, h, g], me_s, sib).wait_recv()
-            acc[:, lanes] += dot(dense[src], mixed[h, src])
-        total[...] += dot(acc[:, lanes].astype(BF16), weights[3, lanes, :])
+            value = value + dot(dense[src], mixed[h, src])
+        last = dot(value.astype(BF16), weights[3, lanes(h), :])
+        if h + 1 < parts:
+            total[...] += last
+        else:
+            out[0] = (total[...] + last).astype(BF16)
 
     loads[2].wait()
     loads[3].wait()
     send_group(0, 0)
     send_group(0, 1)
-    pass_group(0, 0)
-    send_group(1, 0)
-    pass_group(0, 1)
-    near_part(0)
-    send_group(1, 1)
-    pass_group(1, 0)
-    far_part(0)
-    pass_group(1, 1)
-    near_part(1)
-    far_part(1)
-    out[0] = jnp.maximum(total[...], 0.0).astype(BF16)
+    for h in range(parts):
+        pass_group(h, 0)
+        if h + 1 < parts:
+            send_group(h + 1, 0)
+        pass_group(h, 1)
+        near_part(h)
+        if h + 1 < parts:
+            send_group(h + 1, 1)
+        far_part(h)
     for copy in sent:
         copy.wait_send()
 
@@ -297,13 +308,11 @@
     _, rows, width = features.shape
     _, per, slots, tile, _ = tile_values.shape
     ny = nv // 2
-    cols = width // HALVES
-    piece_rows = max(rows // n, 16)
-    piece_cols = cols // (n // (rows // piece_rows))
+    parts, cols, _, piece_rows, piece_cols = cut(n, rows, width)
     taps = rest[2].shape[0]
     dma = pltpu.SemaphoreType.DMA
     hbm = pl.BlockSpec(memory_space=pltpu.HBM)
-    return pl.pallas_call(
+    summed = pl.pallas_call(
         functools.partial(kernel, (n, nv, rows, width, slots, tile)),
         out_shape=jax.ShapeDtypeStruct((1, rows, width), BF16),
         in_specs=[hbm] * 9,
@@ -311,38 +320,41 @@
         scratch_shapes=[
             pltpu.SMEM((per, slots), jnp.int32),
             pltpu.SMEM((1, per), jnp.int32),
-            pltpu.VMEM((nv, rows, width), BF16),
+            pltpu.VMEM((rows, width), BF16),
+            pltpu.VMEM((parts, nv, rows, cols), BF16),
             pltpu.VMEM((per, slots, tile, tile), BF16),
             pltpu.VMEM((nv, rows, rows), BF16),
             pltpu.VMEM((4, width, width), BF16),
             pltpu.VMEM((taps, width), F32),
             pltpu.VMEM((rows, width), F32),
             pltpu.VMEM((rows, width), F32),
-            pltpu.VMEM((HALVES, rows, cols), BF16),
-            pltpu.VMEM((HALVES, n, piece_rows, piece_cols), BF16),
-            pltpu.VMEM((HALVES, n, piece_rows, piece_cols), BF16),
-            pltpu.VMEM((HALVES, nv, rows, cols), BF16),
+            pltpu.VMEM((parts, rows, cols), BF16),
+            pltpu.VMEM((parts, n, piece_rows, piece_cols), BF16),
+            pltpu.VMEM((parts, n, piece_rows, piece_cols), BF16),
+            pltpu.VMEM((parts, nv, rows, cols), BF16),
             dma((9,)),
-            dma((2,)),
-            dma((ny, CHUNKS)),
-            dma((ny, CHUNKS)),
-            dma((ny, CHUNKS)),
-            dma((ny, CHUNKS)),
-            dma((HALVES, n)),
-            dma((HALVES, n)),
-            dma((HALVES, n)),
-            dma((HALVES, n)),
-            dma((ny, HALVES, GROUPS)),
-            dma((ny, HALVES, GROUPS)),
-            dma((HALVES, GROUPS)),
-            dma((HALVES, GROUPS)),
-            dma((ny, HALVES, GROUPS)),
-            dma((ny, HALVES, GROUPS)),
+            dma((parts,)),
+            dma((parts,)),
+            dma((ny, parts)),
+            dma((ny, parts)),
+            dma((ny, parts)),
+            dma((ny, parts)),
+            dma((parts, n)),
+            dma((parts, n)),
+            dma((parts, n)),
+            dma((parts, n)),
+            dma((ny, parts, GROUPS)),
+            dma((ny, parts, GROUPS)),
+            dma((parts, GROUPS)),
+            dma((parts, GROUPS)),
+            dma((ny, parts, GROUPS)),
+            dma((ny, parts, GROUPS)),
         ],
         compiler_params=pltpu.CompilerParams(
             collective_id=0, has_side_effects=True, vmem_limit_bytes=64 * 1024 * 1024
         ),
     )(features, tile_values, tile_column, tile_count, *rest)
+    return jnp.maximum(summed, 0)
 
 
 def solution(mesh):

time: 38.6 us -> 40.8 us (1.057)
  Pallas kernels: 36.8 us -> 39 us
  other arithmetic: 0 us -> 1.67 us
  local copies, waits for them, and re-layouts: 1.67 us -> 0 us
    pallas_call x1, Pallas kernels: 36.8 us -> 39 us  [shards(): pl.pallas_call(functools.partial(kernel, (n, nv, rows, width, slots, tile...]
    max x0 -> x1, other arithmetic: none -> 1.67 us  [shards(): return jnp.maximum(summed, 0)]
    unnamed x1 -> x0, local copies, waits for them, and re-layouts: 1.67 us -> none
where the time goes in v3:
time: 40.8 us; the launch traced here: 40.6 us
  Pallas kernels  39 us (96%)
  other arithmetic  1.67 us (4%)
    pallas_call x1, Pallas kernels, shards(): pl.pallas_call(functools.partial(kernel, (n, nv, rows, width, slots, tile...  39 us
    max x1, other arithmetic, shards(): return jnp.maximum(summed, 0)  1.67 us

profile of v3, /device:TPU:1, one launch (start us, length us, event | category | flops | bytes accessed | tf_op | source)
XLA Modules:
  0.0 40.6 jit_solution(2072620148426357675)
XLA Ops:
  0.0 39.0 %shard_map.91 = bf16[1,256,512]{2,1,0:T(8,128)(2,1)} custom-call(bf16[1,256,512]{2,1,0:T(8,128)(2,1)} %features.1, bf16[1,2,12,128,128]{4,3,2,1,0:T(8,128)(2,1)} %tile_values.1, s32[1,2,12]{2,1,0:T(2,128)} %columns.1, s32[1,2]{1,0:T(1,128)} %counts.1, bf16[512,512]{1,0:T(8,128)(2,1)} %message_one.1, bf16[512,512]{1,0:T(8,128)(2,1)} %root_one.1, ...), custom_call_target="tpu_custom_call" | custom-call | tf_op jit(solution)/shard_map/pallas_call | solution.py:315
  39.0 1.7 %broadcast_maximum_fusion = bf16[1,256,512]{2,1,0:T(8,128)(2,1)} fusion(bf16[1,256,512]{2,1,0:T(8,128)(2,1)} %shard_map.91), kind=kLoop, calls=%fused_computation | loop fusion | flops 131072 | bytes 524288 | tf_op jit(solution)/shard_map/max | solution.py:357

commit v4 on v3

--- a/solution.py
+++ b/solution.py
@@ -9,7 +9,7 @@
 
 MESH = pl.DeviceIdType.MESH
 GROUPS = 2
-MOST_PARTS = 4
+MOST_PARTS = 2
 F32 = jnp.float32
 BF16 = jnp.bfloat16
 

time: 40.8 us -> 36.9 us (0.904)
  Pallas kernels: 39 us -> 35 us
    pallas_call x1, Pallas kernels: 39 us -> 35 us  [shards(): pl.pallas_call(functools.partial(kernel, (n, nv, rows, width, slots, tile...]
where the time goes in v4:
time: 36.9 us; the launch traced here: 36.7 us
  Pallas kernels  35 us (95%)
  other arithmetic  1.67 us (5%)
    pallas_call x1, Pallas kernels, shards(): pl.pallas_call(functools.partial(kernel, (n, nv, rows, width, slots, tile...  35 us
    max x1, other arithmetic, shards(): return jnp.maximum(summed, 0)  1.67 us

profile of v4, /device:TPU:1, one launch (start us, length us, event | category | flops | bytes accessed | tf_op | source)
XLA Modules:
  0.0 36.7 jit_solution(17165929891641877963)
XLA Ops:
  0.0 35.0 %shard_map.91 = bf16[1,256,512]{2,1,0:T(8,128)(2,1)} custom-call(bf16[1,256,512]{2,1,0:T(8,128)(2,1)} %features.1, bf16[1,2,12,128,128]{4,3,2,1,0:T(8,128)(2,1)} %tile_values.1, s32[1,2,12]{2,1,0:T(2,128)} %columns.1, s32[1,2]{1,0:T(1,128)} %counts.1, bf16[512,512]{1,0:T(8,128)(2,1)} %message_one.1, bf16[512,512]{1,0:T(8,128)(2,1)} %root_one.1, ...), custom_call_target="tpu_custom_call" | custom-call | tf_op jit(solution)/shard_map/pallas_call | solution.py:315
  35.0 1.7 %broadcast_maximum_fusion = bf16[1,256,512]{2,1,0:T(8,128)(2,1)} fusion(bf16[1,256,512]{2,1,0:T(8,128)(2,1)} %shard_map.91), kind=kLoop, calls=%fused_computation | loop fusion | flops 131072 | bytes 524288 | tf_op jit(solution)/shard_map/max | solution.py:357

commit v5 on v4

--- a/solution.py
+++ b/solution.py
@@ -100,6 +100,19 @@
         copy.start()
         sent.append(copy)
 
+    def pieces_arrived(h, count, recv):
+        block = by_time.at[h, pl.ds(0, count)]
+        remote(block, block, recv, recv, me_s, sib).wait_recv()
+
+    def pieces_left(h, send):
+        block = by_time.at[h, pl.ds(0, n - 1)]
+        remote(block, block, send, send, me_s, sib).wait_send()
+
+    def all_left():
+        for copy in sent:
+            copy.wait_send()
+        sent.clear()
+
     def y_to(d):
         return ((y + d) % ny) * 2 + core
 
@@ -191,15 +204,12 @@
         for d in order:
             p = flip(me_s, d)
             r, c = piece(p)
-            go(hid.at[h, r, c], by_time.at[h, me_s], p2_send.at[h, d], p2_recv.at[h, d], p, me_v)
+            remote(hid.at[h, r, c], by_time.at[h, me_s], p2_send.at[h], p2_recv.at[h], p, me_v).start()
 
     def filter_part(h):
         r, c = piece(me_s)
         by_time[h, me_s] = hid[h, r, c]
-        for d in range(1, n):
-            p = flip(me_s, d)
-            block = by_time.at[h, p]
-            remote(block, block, p2_send.at[h, d], p2_recv.at[h, d], p, me_v).wait_recv()
+        pieces_arrived(h, n - 1, p2_recv.at[h])
         shift = 0 if across == 1 else (me_s % across) * piece_cols
         for i in range(0, piece_rows, 16):
             for j in range(0, piece_cols, 128):
@@ -215,7 +225,9 @@
                     mix[h, t, i : i + 16, j : j + 128] = value.astype(BF16)
         for d in order:
             p = flip(me_s, d)
-            go(mix.at[h, p], mixed.at[h, me_v, r, c], p3_send.at[h, d], p3_recv.at[h, d], p, me_v)
+            remote(
+                mix.at[h, p], mixed.at[h, me_v, r, c], p3_send.at[h], p3_recv.at[h, d // (n // GROUPS)], p, me_v
+            ).start()
         mixed[h, me_v, r, c] = mix[h, me_s]
 
     pass_on(0)
@@ -240,16 +252,13 @@
         return pl.ds(pl.multiple_of(start * half, half), half)
 
     def send_group(h, g):
-        for d in range(g * size, (g + 1) * size):
-            if d > 0:
-                p = flip(me_s, d)
-                r, c = piece(p)
-                block = mixed.at[h, me_v, r, c]
-                remote(block, block, p3_send.at[h, d], p3_recv.at[h, d], p, me_v).wait_recv()
+        pieces_arrived(h, size if g else size - 1, p3_recv.at[h, g])
         block = mixed.at[h, me_v, group_rows(g)]
         for d in range(1, ny):
             go(block, block, y4_send.at[d, h, g], y4_recv.at[d, h, g], me_s, y_to(d))
-        go(block, block, s4_send.at[h, g], s4_recv.at[h, g], me_s, sib)
+        if g + 1 == GROUPS:
+            block = mixed.at[h, me_v]
+            go(block, block, s4_send.at[h], s4_recv.at[h], me_s, sib)
 
     def pass_group(h, g):
         for d in range(1, ny):
@@ -260,9 +269,8 @@
 
     def near_part(h):
         value = dot(dense[me_v], mixed[h, me_v])
-        for g in range(GROUPS):
-            block = mixed.at[h, sib, group_rows(g)]
-            remote(block, block, s4_send.at[h, g], s4_recv.at[h, g], me_s, sib).wait_recv()
+        block = mixed.at[h, sib]
+        remote(block, block, s4_send.at[h], s4_recv.at[h], me_s, sib).wait_recv()
         acc[:, lanes(h)] = value + dot(dense[sib], mixed[h, sib])
         own = dot(mixed[h, me_v], weights[2, lanes(h), :])
         if h == 0:
@@ -289,6 +297,9 @@
 
     loads[2].wait()
     loads[3].wait()
+    all_left()
+    for h in range(parts):
+        pieces_left(h, p2_send.at[h])
     send_group(0, 0)
     send_group(0, 1)
     for h in range(parts):
@@ -299,9 +310,10 @@
         near_part(h)
         if h + 1 < parts:
             send_group(h + 1, 1)
+            pieces_left(h, p3_send.at[h])
         far_part(h)
-    for copy in sent:
-        copy.wait_send()
+    pieces_left(parts - 1, p3_send.at[parts - 1])
+    all_left()
 
 
 def shards(n, nv, features, tile_values, tile_column, tile_count, *rest):
@@ -339,14 +351,14 @@
             dma((ny, parts)),
             dma((ny, parts)),
             dma((ny, parts)),
-            dma((parts, n)),
-            dma((parts, n)),
-            dma((parts, n)),
-            dma((parts, n)),
+            dma((parts,)),
+            dma((parts,)),
+            dma((parts,)),
+            dma((parts, GROUPS)),
             dma((ny, parts, GROUPS)),
             dma((ny, parts, GROUPS)),
-            dma((parts, GROUPS)),
-            dma((parts, GROUPS)),
+            dma((parts,)),
+            dma((parts,)),
             dma((ny, parts, GROUPS)),
             dma((ny, parts, GROUPS)),
         ],

time: 36.9 us -> 36.3 us (0.984)
  Pallas kernels: 35 us -> 34.5 us
    pallas_call x1, Pallas kernels: 35 us -> 34.5 us  [shards(): pl.pallas_call(functools.partial(kernel, (n, nv, rows, width, slots, tile...]
where the time goes in v5:
time: 36.3 us; the launch traced here: 36.2 us
  Pallas kernels  34.5 us (95%)
  other arithmetic  1.67 us (5%)
    pallas_call x1, Pallas kernels, shards(): pl.pallas_call(functools.partial(kernel, (n, nv, rows, width, slots, tile...  34.5 us
    max x1, other arithmetic, shards(): return jnp.maximum(summed, 0)  1.67 us

profile of v5, /device:TPU:1, one launch (start us, length us, event | category | flops | bytes accessed | tf_op | source)
XLA Modules:
  0.0 36.2 jit_solution(16820915029060274346)
XLA Ops:
  0.0 34.5 %shard_map.91 = bf16[1,256,512]{2,1,0:T(8,128)(2,1)} custom-call(bf16[1,256,512]{2,1,0:T(8,128)(2,1)} %features.1, bf16[1,2,12,128,128]{4,3,2,1,0:T(8,128)(2,1)} %tile_values.1, s32[1,2,12]{2,1,0:T(2,128)} %columns.1, s32[1,2]{1,0:T(1,128)} %counts.1, bf16[512,512]{1,0:T(8,128)(2,1)} %message_one.1, bf16[512,512]{1,0:T(8,128)(2,1)} %root_one.1, ...), custom_call_target="tpu_custom_call" | custom-call | tf_op jit(solution)/shard_map/pallas_call | solution.py:327
  34.5 1.7 %broadcast_maximum_fusion = bf16[1,256,512]{2,1,0:T(8,128)(2,1)} fusion(bf16[1,256,512]{2,1,0:T(8,128)(2,1)} %shard_map.91), kind=kLoop, calls=%fused_computation | loop fusion | flops 131072 | bytes 524288 | tf_op jit(solution)/shard_map/max | solution.py:369

commit v6 on v5

--- a/solution.py
+++ b/solution.py
@@ -128,15 +128,16 @@
     load_taps = pltpu.make_async_copy(time_taps, taps, local_sem.at[6])
     load_columns = pltpu.make_async_copy(columns.at[0], column_smem, local_sem.at[7])
     load_counts = pltpu.make_async_copy(counts, count_smem, local_sem.at[8])
-    for load in (load_feats, loads[1], load_columns, load_counts, load_tiles, loads[0], load_taps, loads[2], loads[3]):
-        load.start()
-
+    load_feats.start()
+    loads[1].start()
     barrier = pltpu.get_barrier_semaphore()
     for d in range(1, n):
         pl.semaphore_signal(barrier, inc=1, device_id=(flip(me_s, d), me_v), device_id_type=MESH)
     for d in range(1, ny):
         pl.semaphore_signal(barrier, inc=1, device_id=(me_s, y_to(d)), device_id_type=MESH)
     pl.semaphore_signal(barrier, inc=1, device_id=(me_s, sib), device_id_type=MESH)
+    for load in (load_columns, load_counts, load_tiles, loads[0], load_taps, loads[2], loads[3]):
+        load.start()
 
     def dot(a, b):
         return jnp.dot(a, b, preferred_element_type=F32)
@@ -230,15 +231,11 @@
             ).start()
         mixed[h, me_v, r, c] = mix[h, me_s]
 
-    pass_on(0)
-    near_messages(0)
     load_taps.wait()
     for h in range(parts):
-        if h + 1 < parts:
-            pass_on(h + 1)
+        pass_on(h)
+        near_messages(h)
         far_messages(h)
-        if h + 1 < parts:
-            near_messages(h + 1)
         if h >= 2:
             filter_part(h - 2)
     for h in range(max(0, parts - 2), parts):
@@ -306,12 +303,16 @@
         pass_group(h, 0)
         if h + 1 < parts:
             send_group(h + 1, 0)
+        if h > 0:
+            far_part(h - 1)
+            near_part(h)
         pass_group(h, 1)
-        near_part(h)
         if h + 1 < parts:
             send_group(h + 1, 1)
             pieces_left(h, p3_send.at[h])
-        far_part(h)
+        if h == 0:
+            near_part(h)
+    far_part(parts - 1)
     pieces_left(parts - 1, p3_send.at[parts - 1])
     all_left()
 
@@ -324,6 +325,7 @@
     taps = rest[2].shape[0]
     dma = pltpu.SemaphoreType.DMA
     hbm = pl.BlockSpec(memory_space=pltpu.HBM)
+    hold = [pltpu.with_memory_space_constraint(x, pltpu.HBM) for x in (features, tile_values, tile_column, tile_count, *rest)]
     summed = pl.pallas_call(
         functools.partial(kernel, (n, nv, rows, width, slots, tile)),
         out_shape=jax.ShapeDtypeStruct((1, rows, width), BF16),
@@ -363,9 +365,9 @@
             dma((ny, parts, GROUPS)),
         ],
         compiler_params=pltpu.CompilerParams(
-            collective_id=0, has_side_effects=True, vmem_limit_bytes=64 * 1024 * 1024
+            collective_id=0, has_side_effects=True, vmem_limit_bytes=40 * 1024 * 1024
         ),
-    )(features, tile_values, tile_column, tile_count, *rest)
+    )(*hold)
     return jnp.maximum(summed, 0)
 
 

time: 36.3 us -> 34 us (0.937)
  Pallas kernels: 34.5 us -> 33.1 us
  other arithmetic: 1.67 us -> 0.72 us
    pallas_call x1, Pallas kernels: 34.5 us -> 33.1 us  [shards(): pl.pallas_call(functools.partial(kernel, (n, nv, rows, width, slots, tile...]
    max x1, other arithmetic: 1.67 us -> 0.72 us  [shards(): return jnp.maximum(summed, 0)]
where the time goes in v6:
time: 34 us; the launch traced here: 33.9 us
  Pallas kernels  33.1 us (97%)
  other arithmetic  0.72 us (2%)
    pallas_call x1, Pallas kernels, shards(): pl.pallas_call(functools.partial(kernel, (n, nv, rows, width, slots, tile...  33.1 us
    max x1, other arithmetic, shards(): return jnp.maximum(summed, 0)  0.72 us

profile of v6, /device:TPU:1, one launch (start us, length us, event | category | flops | bytes accessed | tf_op | source)
XLA Modules:
  0.0 33.9 jit_solution(5983347763651786066)
XLA Ops:
  0.0 33.1 %shard_map.91 = bf16[1,256,512]{2,1,0:T(8,128)(2,1)S(1)} custom-call(bf16[1,256,512]{2,1,0:T(8,128)(2,1)} %features.1, bf16[1,2,12,128,128]{4,3,2,1,0:T(8,128)(2,1)} %tile_values.1, s32[1,2,12]{2,1,0:T(2,128)} %columns.1, s32[1,2]{1,0:T(1,128)} %counts.1, bf16[512,512]{1,0:T(8,128)(2,1)} %message_one.1, bf16[512,512]{1,0:T(8,128)(2,1)} %root_one.1, ...), custom_call_target="tpu_custom_call" | custom-call | tf_op jit(solution)/shard_map/pallas_call | solution.py:329
  33.1 0.7 %broadcast_maximum_fusion = bf16[1,256,512]{2,1,0:T(8,128)(2,1)} fusion(bf16[1,256,512]{2,1,0:T(8,128)(2,1)S(1)} %shard_map.91), kind=kLoop, calls=%fused_computation | loop fusion | flops 131072 | bytes 524288 | tf_op jit(solution)/shard_map/max | solution.py:371

commit v7 on v6

--- a/solution.py
+++ b/solution.py
@@ -170,7 +170,8 @@
         [jnp.where(k < count_smem[0, b], column_smem[b, k], -1) for k in range(slots)] for b in range(per)
     ]
 
-    def fill(v, carry):
+    def fill(i, carry):
+        v = ((y - i // 2 + ny) % ny) * 2 + (core + i) % 2
         for b in range(per):
             for j in range(per):
                 block = jnp.zeros((tile, tile), F32)
@@ -180,7 +181,7 @@
                 dense[v, b * tile : (b + 1) * tile, j * tile : (j + 1) * tile] = block.astype(BF16)
         return carry
 
-    lax.fori_loop(0, nv, fill, 0)
+    lax.fori_loop(0, 2, fill, 0)
 
     order = list(range(n // 2, n)) + list(range(1, n // 2))
     loads[0].wait()
@@ -234,6 +235,8 @@
     load_taps.wait()
     for h in range(parts):
         pass_on(h)
+        if h == 0:
+            lax.fori_loop(2, nv, fill, 0)
         near_messages(h)
         far_messages(h)
         if h >= 2:
@@ -305,13 +308,11 @@
             send_group(h + 1, 0)
         if h > 0:
             far_part(h - 1)
-            near_part(h)
         pass_group(h, 1)
         if h + 1 < parts:
             send_group(h + 1, 1)
             pieces_left(h, p3_send.at[h])
-        if h == 0:
-            near_part(h)
+        near_part(h)
     far_part(parts - 1)
     pieces_left(parts - 1, p3_send.at[parts - 1])
     all_left()

time: 34 us -> 33.4 us (0.982)
  Pallas kernels: 33.1 us -> 32.6 us
    pallas_call x1, Pallas kernels: 33.1 us -> 32.6 us  [shards(): pl.pallas_call(functools.partial(kernel, (n, nv, rows, width, slots, tile...]
where the time goes in v7:
time: 33.4 us; the launch traced here: 33.3 us
  Pallas kernels  32.6 us (98%)
  other arithmetic  0.72 us (2%)
    pallas_call x1, Pallas kernels, shards(): pl.pallas_call(functools.partial(kernel, (n, nv, rows, width, slots, tile...  32.6 us
    max x1, other arithmetic, shards(): return jnp.maximum(summed, 0)  0.72 us

profile of v7, /device:TPU:1, one launch (start us, length us, event | category | flops | bytes accessed | tf_op | source)
XLA Modules:
  0.0 33.3 jit_solution(8657094692533197473)
XLA Ops:
  0.0 32.6 %shard_map.91 = bf16[1,256,512]{2,1,0:T(8,128)(2,1)S(1)} custom-call(bf16[1,256,512]{2,1,0:T(8,128)(2,1)} %features.1, bf16[1,2,12,128,128]{4,3,2,1,0:T(8,128)(2,1)} %tile_values.1, s32[1,2,12]{2,1,0:T(2,128)} %columns.1, s32[1,2]{1,0:T(1,128)} %counts.1, bf16[512,512]{1,0:T(8,128)(2,1)} %message_one.1, bf16[512,512]{1,0:T(8,128)(2,1)} %root_one.1, ...), custom_call_target="tpu_custom_call" | custom-call | tf_op jit(solution)/shard_map/pallas_call | solution.py:330
  32.6 0.7 %broadcast_maximum_fusion = bf16[1,256,512]{2,1,0:T(8,128)(2,1)} fusion(bf16[1,256,512]{2,1,0:T(8,128)(2,1)S(1)} %shard_map.91), kind=kLoop, calls=%fused_computation | loop fusion | flops 131072 | bytes 524288 | tf_op jit(solution)/shard_map/max | solution.py:372

commit v8 on v7

--- a/solution.py
+++ b/solution.py
@@ -8,7 +8,7 @@
 from jax.sharding import PartitionSpec as P
 
 MESH = pl.DeviceIdType.MESH
-GROUPS = 2
+GROUPS = 4
 MOST_PARTS = 2
 F32 = jnp.float32
 BF16 = jnp.bfloat16
@@ -248,7 +248,7 @@
     size = n // GROUPS
 
     def group_rows(g):
-        start = me_s // size if g == 0 else 1 - me_s // size
+        start = flip(me_s // size, g)
         return pl.ds(pl.multiple_of(start * half, half), half)
 
     def send_group(h, g):
@@ -300,19 +300,18 @@
     all_left()
     for h in range(parts):
         pieces_left(h, p2_send.at[h])
-    send_group(0, 0)
-    send_group(0, 1)
-    for h in range(parts):
-        pass_group(h, 0)
-        if h + 1 < parts:
-            send_group(h + 1, 0)
-        if h > 0:
-            far_part(h - 1)
-        pass_group(h, 1)
-        if h + 1 < parts:
-            send_group(h + 1, 1)
-            pieces_left(h, p3_send.at[h])
-        near_part(h)
+    steps = [(h, g) for h in range(parts) for g in range(GROUPS)]
+    for i in range(len(steps) + 2):
+        if i < len(steps):
+            send_group(*steps[i])
+        if i >= 2:
+            h, g = steps[i - 2]
+            pass_group(h, g)
+            if g + 1 == GROUPS:
+                near_part(h)
+            elif g == 1 and h > 0:
+                far_part(h - 1)
+                pieces_left(h - 1, p3_send.at[h - 1])
     far_part(parts - 1)
     pieces_left(parts - 1, p3_send.at[parts - 1])
     all_left()

time: 33.4 us -> 34.3 us (1.027)
  Pallas kernels: 32.6 us -> 33.5 us
    pallas_call x1, Pallas kernels: 32.6 us -> 33.5 us  [shards(): pl.pallas_call(functools.partial(kernel, (n, nv, rows, width, slots, tile...]
where the time goes in v8:
time: 34.3 us; the launch traced here: 34.2 us
  Pallas kernels  33.5 us (98%)
  other arithmetic  0.72 us (2%)
    pallas_call x1, Pallas kernels, shards(): pl.pallas_call(functools.partial(kernel, (n, nv, rows, width, slots, tile...  33.5 us
    max x1, other arithmetic, shards(): return jnp.maximum(summed, 0)  0.72 us

profile of v8, /device:TPU:1, one launch (start us, length us, event | category | flops | bytes accessed | tf_op | source)
XLA Modules:
  0.0 34.2 jit_solution(6129663654881234780)
XLA Ops:
  0.0 33.5 %shard_map.91 = bf16[1,256,512]{2,1,0:T(8,128)(2,1)S(1)} custom-call(bf16[1,256,512]{2,1,0:T(8,128)(2,1)} %features.1, bf16[1,2,12,128,128]{4,3,2,1,0:T(8,128)(2,1)} %tile_values.1, s32[1,2,12]{2,1,0:T(2,128)} %columns.1, s32[1,2]{1,0:T(1,128)} %counts.1, bf16[512,512]{1,0:T(8,128)(2,1)} %message_one.1, bf16[512,512]{1,0:T(8,128)(2,1)} %root_one.1, ...), custom_call_target="tpu_custom_call" | custom-call | tf_op jit(solution)/shard_map/pallas_call | solution.py:329
  33.5 0.7 %broadcast_maximum_fusion = bf16[1,256,512]{2,1,0:T(8,128)(2,1)} fusion(bf16[1,256,512]{2,1,0:T(8,128)(2,1)S(1)} %shard_map.91), kind=kLoop, calls=%fused_computation | loop fusion | flops 131072 | bytes 524288 | tf_op jit(solution)/shard_map/max | solution.py:371

commit v9 on v7

--- a/solution.py
+++ b/solution.py
@@ -175,9 +175,12 @@
         for b in range(per):
             for j in range(per):
                 block = jnp.zeros((tile, tile), F32)
-                for k in range(slots):
-                    scale = jnp.where(live[b][k] == v * per + j, 1.0, 0.0).astype(F32)
-                    block = block + scale * tiles[b, k].astype(F32)
+                for k in range(0, slots, 2):
+                    pair = jnp.zeros((tile, tile), BF16)
+                    for m in range(k, min(k + 2, slots)):
+                        scale = jnp.where(live[b][m] == v * per + j, 1.0, 0.0).astype(F32)
+                        pair = pair + jnp.full((tile, tile), scale, F32).astype(BF16) * tiles[b, m]
+                    block = block + pair.astype(F32)
                 dense[v, b * tile : (b + 1) * tile, j * tile : (j + 1) * tile] = block.astype(BF16)
         return carry
 

time: 33.4 us -> 33.4 us (level)
  no operation moved by 1% of the time
where the time goes in v9:
time: 33.4 us; the launch traced here: 33.3 us
  Pallas kernels  32.6 us (98%)
  other arithmetic  0.72 us (2%)
    pallas_call x1, Pallas kernels, shards(): pl.pallas_call(functools.partial(kernel, (n, nv, rows, width, slots, tile...  32.6 us
    max x1, other arithmetic, shards(): return jnp.maximum(summed, 0)  0.72 us

profile of v9, /device:TPU:1, one launch (start us, length us, event | category | flops | bytes accessed | tf_op | source)
XLA Modules:
  0.0 33.3 jit_solution(3847362325660545914)
XLA Ops:
  0.0 32.6 %shard_map.91 = bf16[1,256,512]{2,1,0:T(8,128)(2,1)S(1)} custom-call(bf16[1,256,512]{2,1,0:T(8,128)(2,1)} %features.1, bf16[1,2,12,128,128]{4,3,2,1,0:T(8,128)(2,1)} %tile_values.1, s32[1,2,12]{2,1,0:T(2,128)} %columns.1, s32[1,2]{1,0:T(1,128)} %counts.1, bf16[512,512]{1,0:T(8,128)(2,1)} %message_one.1, bf16[512,512]{1,0:T(8,128)(2,1)} %root_one.1, ...), custom_call_target="tpu_custom_call" | custom-call | tf_op jit(solution)/shard_map/pallas_call | solution.py:333
  32.6 0.7 %broadcast_maximum_fusion = bf16[1,256,512]{2,1,0:T(8,128)(2,1)} fusion(bf16[1,256,512]{2,1,0:T(8,128)(2,1)S(1)} %shard_map.91), kind=kLoop, calls=%fused_computation | loop fusion | flops 131072 | bytes 524288 | tf_op jit(solution)/shard_map/max | solution.py:375
